TPU v7x, 32 devices: a whole 2x2x4 slice. The times are simulated.
32 devices in a mesh: groups: 2 (over y), age: 4 (over z), span: 2 (over x), blade: 2 (over core).
Axes of the slice: x: 2, y: 2, z: 4, core: 2. Of those that a mesh axis runs over, the one named last changes fastest.
Arguments:
- surface_mu: float32 [32, 4, 64, 128], P(('groups', 'age'), 'blade', None, 'span'), parts along dimension 0, may hold values from -6 to 6
- centroid_body: float32 [3, 4, 64, 128], P(None, 'blade', None, 'span'), may hold values from -0.04 to 1.01
- area_normal: float32 [3, 4, 64, 128], P(None, 'blade', None, 'span'), may hold values from -0.12 to 0.12
- te_body: float32 [3, 4, 128], P(None, 'blade', 'span'), may hold values from -0.04 to 1.01
- wake_state: float32 [4, 4, 64, 2, 128], P(None, 'blade', ('groups', 'age'), 'span'), parts along dimension 2, may hold values from -2 to 2
- pairs: int32 [4, 64, 2, 8], P('blade', ('groups', 'age'), 'span'), parts along dimension 1, may hold values from -1 to 71, as said below
- az_index: int32 [6], P('groups'), parts along dimension 0, may hold values from 0 to 15
- free_stream: float32 [6], P('groups'), parts along dimension 0, may hold values from -3 to 3
Outputs:
- wake_final: float32 [4, 4, 64, 2, 128], P(None, 'blade', ('groups', 'age'), 'span'), parts along dimension 2
- wake_velocity: float32 [3, 4, 64, 2, 128], P(None, 'blade', ('groups', 'age'), 'span'), parts along dimension 2
There are 2 independent parts, one for each index of `groups`. A program takes and returns all parts, laid end to end along the dimension named above; an argument that names none is the same for every part. Nothing has to cross between parts.
Inputs may be any that keep to these rules, and one draw needn't show every extreme that they name: Rows come in age blocks of 16 rows (8 tiles), spanwise panels in strips of 64. An entry v >= 0 of pairs[b, t, s, :] names tile v % 8 of age block t // 8 + v // 24 - 1 in strip s + (v // 8) % 3 - 1 of the same blade; -1 marks an empty slot. In each aligned block of 2 blades, one age block and one strip, at most 64 entries are not -1, and exactly 64 in one such block.
All inputs are finite; a program needn't handle non-finite values.
Results may differ from a plain program's by a relative error of at most 0.0003.
Values sent between devices are 32-bit elements; how exact they have to be, the bound alone decides.
A program may use at most 64 MiB of HBM per device.

v0:
```python
import math

import jax
import jax.numpy as jnp
from jax import lax
from jax.sharding import PartitionSpec as P

CB = 8


time_step = 0.05
near_core = 0.0025
far_core = 0.01
inv_four_pi = 0.25 / math.pi


def spread(shard, axis, root):
    mine = lax.axis_index(axis) == root
    return lax.psum(jnp.where(mine, shard, jnp.zeros_like(shard)), axis)


def with_halo(cells, sides, width):
    for axis, dim in sides:
        count = lax.axis_size(axis)
        ends = count - 1
        head = lax.slice_in_dim(cells, 0, width, axis=dim)
        tail = lax.slice_in_dim(cells, cells.shape[dim] - width, cells.shape[dim], axis=dim)
        cells = jnp.concatenate(
            [
                lax.ppermute(tail, axis, [(i, (i + 1) % count) for i in range(ends)]),
                cells,
                lax.ppermute(head, axis, [((i + 1) % count, i) for i in range(ends)]),
            ],
            axis=dim,
        )
    return cells


def shifted(value, axis, steps):
    count = lax.axis_size(axis)
    first, last = (max(0, -steps), min(count, count - steps))
    return lax.ppermute(value, axis, [(source, source + steps) for source in range(first, last)])


def rotate(vector, cosine, sine_val):
    return jnp.stack(
        [
            vector[0] * cosine - vector[1] * sine_val,
            vector[0] * sine_val + vector[1] * cosine,
            vector[2],
        ]
    )


def coarse_sum(values, block_size):
    shape = values.shape
    grouped = values.reshape(
        shape[:-2] + (shape[-2] // block_size, block_size, shape[-1] // block_size, block_size)
    )
    return jnp.sum(grouped, axis=(-3, -1))


def far_velocity(targets, centers, moments):
    separation = targets[:, :, None] - centers[:, None, :]
    dist_sq = jnp.sum(separation * separation, axis=0) + far_core
    inverse = 1.0 / jnp.sqrt(dist_sq)
    inverse_cube = inverse * inverse * inverse
    projection = jnp.sum(moments[:, None, :] * separation, axis=0)
    values = (
        3.0 * projection * inverse_cube * inverse * inverse * separation
        - moments[:, None, :] * inverse_cube
    )
    return inv_four_pi * jnp.sum(values, axis=2)


def near_velocity(targets, sources, strengths):
    separation = targets[:, :, None] - sources[:, None, :]
    dist_sq = jnp.sum(separation * separation, axis=0) + near_core
    weight = 1.0 / (dist_sq * jnp.sqrt(dist_sq))
    cross_prod = jnp.stack(
        [
            strengths[1][None, :] * separation[2] - strengths[2][None, :] * separation[1],
            strengths[2][None, :] * separation[0] - strengths[0][None, :] * separation[2],
            strengths[0][None, :] * separation[1] - strengths[1][None, :] * separation[0],
        ]
    )
    return inv_four_pi * jnp.sum(cross_prod * weight[None], axis=2)


def sheet_strength(pos_pad, mu_pad):
    pos_r = 0.5 * (pos_pad[:, :, 2:, 1:-1] - pos_pad[:, :, :-2, 1:-1])
    pos_s = 0.5 * (pos_pad[:, :, 1:-1, 2:] - pos_pad[:, :, 1:-1, :-2])
    mu_r = 0.5 * (mu_pad[:, 2:, 1:-1] - mu_pad[:, :-2, 1:-1])
    mu_s = 0.5 * (mu_pad[:, 1:-1, 2:] - mu_pad[:, 1:-1, :-2])
    return mu_s[None] * pos_r - mu_r[None] * pos_s


def grouped_map(kernel, operands):
    length = jax.tree.leaves(operands)[0].shape[0]
    turn_count = math.gcd(length, 16)
    shaped = jax.tree.map(
        lambda array: array.reshape((turn_count, length // turn_count) + array.shape[1:]), operands
    )
    result = lax.map(jax.vmap(kernel), shaped)
    return result.reshape((length,) + result.shape[2:])


def far_kernel(centers, moments):

    def apply_one(target_tile):
        return far_velocity(target_tile, centers, moments)

    return apply_one


def near_kernel(bundle):
    return near_velocity(bundle[0], bundle[1], bundle[2])


def on_device(
    surface_mu, centroid_body, area_normal, te_body, wake_state, pairs, az_index, free_stream
):
    az_dev, blade_group, chord_len, span_dev = surface_mu.shape
    tile_dev = wake_state.shape[2]
    lanes = wake_state.shape[4]
    rows_dev = tile_dev * lanes // span_dev
    slot_tile = pairs.shape[3]
    step_count = az_index.shape[0]
    age_count = lax.axis_size("age")
    span_count = lax.axis_size("span")
    blade_count = lax.axis_size("blade")
    age_pos = lax.axis_index("age")
    span_pos = lax.axis_index("span")
    blade_pos = lax.axis_index("blade")
    naz_total = az_dev * age_count
    blade_total = blade_group * blade_count
    tile_local = blade_group * tile_dev
    block_cells = chord_len // CB * (span_dev // CB)
    per_device = blade_group * block_cells
    column = jnp.arange(per_device * span_count * blade_count, dtype=jnp.int32)
    column_blade = (
        column // per_device % blade_count * blade_group + column % per_device // block_cells
    )
    column_frac = column_blade.astype(jnp.float32) / blade_total
    local_frac = (blade_pos * blade_group + jnp.arange(blade_group, dtype=jnp.int32)).astype(
        jnp.float32
    ) / blade_total
    center_local = (coarse_sum(centroid_body, CB) / (CB * CB)).reshape(3, per_device)
    center_all = lax.all_gather(center_local, ("span", "blade"), axis=1, tiled=True)
    sheet_grid = wake_state[:, :, :, 0, :].reshape(4, blade_group, rows_dev, span_dev)
    velocity = jnp.zeros((3, blade_group, tile_dev, lanes), jnp.float32)
    for step_num in range(step_count):
        azimuth = az_index[step_num]
        mu_now = lax.dynamic_index_in_dim(surface_mu, azimuth % az_dev, 0, keepdims=False)
        moment_local = coarse_sum(mu_now[None] * area_normal, CB).reshape(3, per_device)
        trailing_local = (mu_now[:, chord_len - 1, :] - mu_now[:, 0, :]).reshape(
            blade_group * span_dev
        )
        moment_local, trailing_local = (moment_local, trailing_local)
        moment_got, trailing = (
            spread(moment_local, "age", azimuth // az_dev),
            spread(trailing_local, "age", azimuth // az_dev),
        )
        moment_all = lax.all_gather(moment_got, ("span", "blade"), axis=1, tiled=True)
        turn_frac = azimuth.astype(jnp.float32) / naz_total
        source_angle = 2.0 * math.pi * (turn_frac + column_frac)
        source_cos = jnp.cos(source_angle)
        source_sin = jnp.sin(source_angle)
        centers = rotate(center_all, source_cos, source_sin)
        moments = rotate(moment_all, source_cos, source_sin)
        padded = with_halo(sheet_grid, (("age", 2), ("span", 3)), 1)
        pos_pad = padded[:3]
        top_rows = jnp.where(age_pos == 0, pos_pad[:, :, 1, :], pos_pad[:, :, 0, :])
        bottom_rows = jnp.where(
            age_pos == age_count - 1, pos_pad[:, :, -2, :], pos_pad[:, :, -1, :]
        )
        pos_pad = jnp.concatenate(
            [top_rows[:, :, None], pos_pad[:, :, 1:-1], bottom_rows[:, :, None]], 2
        )
        left_cols = jnp.where(span_pos == 0, pos_pad[..., 1], pos_pad[..., 0])
        right_cols = jnp.where(span_pos == span_count - 1, pos_pad[..., -2], pos_pad[..., -1])
        pos_pad = jnp.concatenate(
            [left_cols[..., None], pos_pad[..., 1:-1], right_cols[..., None]], 3
        )
        strength = sheet_strength(pos_pad, padded[3])
        pos_tiles = sheet_grid[:3].reshape(3, blade_group, tile_dev, lanes)
        str_tiles = strength.reshape(3, blade_group, tile_dev, lanes)
        targets = pos_tiles.reshape(3, tile_local, lanes).transpose(1, 0, 2)
        far_field = grouped_map(far_kernel(centers, moments), targets)
        blocks = jnp.concatenate([pos_tiles, str_tiles], 0).transpose(1, 2, 0, 3)[:, None, None]
        beside_all = with_halo(blocks, (("age", 1), ("span", 2)), 1)
        source_table = beside_all.reshape(blade_group, 9 * tile_dev, 6, lanes)
        pair_ids = pairs[:, :, 0, :]
        live_mask = pair_ids >= 0
        safe_ids = jnp.maximum(pair_ids, 0)
        picked = source_table[jnp.arange(blade_group, dtype=jnp.int32)[:, None, None], safe_ids]
        weights = live_mask.astype(jnp.float32)[:, :, :, None, None]
        sources = (
            picked[:, :, :, :3]
            .reshape(tile_local, slot_tile, 3, lanes)
            .transpose(0, 2, 1, 3)
            .reshape(tile_local, 3, slot_tile * lanes)
        )
        strengths = (
            (picked[:, :, :, 3:] * weights)
            .reshape(tile_local, slot_tile, 3, lanes)
            .transpose(0, 2, 1, 3)
            .reshape(tile_local, 3, slot_tile * lanes)
        )
        near_flat = grouped_map(near_kernel, (targets, sources, strengths))
        far_part = far_field.transpose(1, 0, 2).reshape(3, blade_group, tile_dev, lanes)
        near_part = near_flat.transpose(1, 0, 2).reshape(3, blade_group, tile_dev, lanes)
        velocity = free_stream[:, None, None, None] + far_part + near_part
        moved_pos = sheet_grid[:3] + time_step * velocity.reshape(
            3, blade_group, rows_dev, span_dev
        )
        moved_state = jnp.concatenate([moved_pos, sheet_grid[3:4]], 0)
        incoming = shifted(moved_state[:, :, -1, :], "age", 1)
        blade_angle = 2.0 * math.pi * (turn_frac + local_frac)
        te_pos = rotate(te_body, jnp.cos(blade_angle)[:, None], jnp.sin(blade_angle)[:, None])
        shed_row = jnp.concatenate([te_pos, trailing.reshape(1, blade_group, span_dev)], 0)
        incoming = jnp.where(age_pos == 0, shed_row, incoming)
        sheet_grid = jnp.concatenate([incoming[:, :, None, :], moved_state[:, :, :-1, :]], 2)
    final_tiles = sheet_grid.reshape(4, blade_group, tile_dev, lanes)
    return (final_tiles[:, :, :, None, :], velocity[:, :, :, None, :])


def solution(mesh):
    in_specs = (
        P(("groups", "age"), "blade", None, "span"),
        P(None, "blade", None, "span"),
        P(None, "blade", None, "span"),
        P(None, "blade", "span"),
        P(None, "blade", ("groups", "age"), "span", None),
        P("blade", ("groups", "age"), "span", None),
        P("groups"),
        P("groups"),
    )
    out_specs = (
        P(None, "blade", ("groups", "age"), "span", None),
        P(None, "blade", ("groups", "age"), "span", None),
    )
    return jax.shard_map(
        on_device, mesh=mesh, in_specs=in_specs, out_specs=out_specs, check_vma=False
    )
```

profile of v0, /device:TPU:0, one launch (start us, length us, event | category | flops | bytes accessed | tf_op | source)
XLA Modules:
  0.0 256.6 jit_solution(8771473071030211586)
XLA Ops:
  2.7 4.9 %collective-permute-start = (f32[4,2,1,64]{3,1,2,0:T(2,128)S(1)}, f32[4,2,1,64]{3,1,2,0:T(2,128)S(1)}, u32[]{:S(2)}, u32[]{:S(2)}) collective-permute-start(f32[4,2,1,64]{3,1,2,0:T(2,128)S(1)} %copy.303), channel_id=1, source_target_pairs={{0,4},{4,8},{8,12},{1,5},{5,9},{9,13},{2,6},{6,10},{10,14},{3,7},{... | collective-permute-start | bytes 6152 | tf_op jit(solution)/shard_map/ppermute | solution.py:30
  26.2 13.3 %all-reduce = (f32[3,128]{1,0:T(4,128)S(1)}, f32[1,2,64]{2,1,0:T(2,128)S(1)}, f32[3,128]{1,0:T(4,128)S(1)}, f32[1,2,64]{2,1,0:T(2,128)S(1)}, f32[3,128]{1,0:T(4,128)S(1)}, /*index=5*/f32[1,2,64]{2,1,0:T(2,128)S(1)}) all-reduce(f32[3,128]{1,0:T(4,128)S(1)} %select_n.377, ...), channel_id=1, replica_groups=mesh['groups'=2,'age'=4,'span'=2,'blade'=2] {'age'}, use_global_device_ids=true, to_apply=%region_5.6 | all-reduce | flops 1536 | bytes 12288 | tf_op jit(solution)/shard_map/psum | solution.py:19
  39.6 5.2 %all_gather.12 = f32[3,512]{1,0:T(4,128)S(1)} all-gather(f32[3,128]{1,0:T(4,128)S(1)} %get-tuple-element.344), channel_id=1, replica_groups=mesh['groups'=2,'age'=4,'span'=2,'blade'=2] {'span','blade'}, dimensions={1}, use_global_device_ids=true | all-gather | bytes 7680 | tf_op jit(solution)/shard_map/all_gather | solution.py:164
  45.5 5.2 %all_gather.13 = f32[3,512]{1,0:T(4,128)S(1)} all-gather(f32[3,128]{1,0:T(4,128)S(1)} %div.142), channel_id=1, replica_groups=mesh['groups'=2,'age'=4,'span'=2,'blade'=2] {'span','blade'}, dimensions={1}, use_global_device_ids=true | all-gather | bytes 7680 | tf_op jit(solution)/shard_map/all_gather | solution.py:149
  51.0 9.9 %while.60 = (s32[]{:T(128)}, f32[16,1,3,128]{3,2,1,0:T(4,128)S(1)}, f32[3,512]{1,0:T(4,128)S(1)}, f32[16,1,3,128]{3,2,1,0:T(4,128)S(1)}, f32[3,512]{1,0:T(4,128)S(1)}, /*index=5*/s32[]{:T(128)}) while((s32[]{:T(128)}, f32[16,1,3,128]{3,2,1,0:T(4,128)S(1)}, f32[3,512]{1,0:T(4,128)S(1)}, f32[16,1,3,128]{3,2,1,0:T(4,128)S(1)}, ...), condition=%wide.region_10.11_spmd, body=%wide.region_6.10_spmd.sunk | while | flops 2293762 | bytes 2133589 | solution.py:104
  60.9 5.2 %all_gather.14 = f32[3,512]{1,0:T(4,128)S(1)} all-gather(f32[3,128]{1,0:T(4,128)S(1)} %get-tuple-element.346), channel_id=1, replica_groups=mesh['groups'=2,'age'=4,'span'=2,'blade'=2] {'span','blade'}, dimensions={1}, use_global_device_ids=true | all-gather | bytes 7680 | tf_op jit(solution)/shard_map/all_gather | solution.py:164
  68.5 4.5 %collective-permute-start.2 = (f32[4,2,18,1]{3,1,2,0:T(2,128)S(1)}, f32[4,2,18,1]{3,1,2,0:T(2,128)S(1)}, u32[]{:S(2)}, u32[]{:S(2)}) collective-permute-start(f32[4,2,18,1]{3,1,2,0:T(2,128)S(1)} %get-tuple-element.398), channel_id=1, source_target_pairs={{0,2},{1,3},{4,6},{5,7},{8,10},{9,11},{12,14},{13,15},{16,18},{17,... | collective-permute-start | bytes 1736 | tf_op jit(solution)/shard_map/ppermute | solution.py:30
  77.7 4.5 %collective-permute-start.4 = (f32[2,1,1,8,6,128]{5,3,0,4,2,1:T(8,128)S(1)}, f32[2,1,1,8,6,128]{5,3,0,4,2,1:T(8,128)S(1)}, u32[]{:S(2)}, u32[]{:S(2)}) collective-permute-start(f32[2,1,1,8,6,128]{5,3,0,4,2,1:T(8,128)S(1)} %maximum_bitcast_fusion.3), channel_id=1, source_target_pairs={{0,4},{4,8},{8,12},{1,5},{5,9},{9,13},{2,6},{6,10},{10,14},{3,7},{... | collective-permute-start | bytes 147464 | tf_op jit(solution)/shard_map/ppermute | solution.py:30
  85.3 4.6 %collective-permute-start.6 = (f32[2,3,1,8,6,128]{5,3,0,4,2,1:T(8,128)S(1)}, f32[2,3,1,8,6,128]{5,3,0,4,2,1:T(8,128)S(1)}, u32[]{:S(2)}, u32[]{:S(2)}) collective-permute-start(f32[2,3,1,8,6,128]{5,3,0,4,2,1:T(8,128)S(1)} %pad_maximum_fusion.3), channel_id=1, source_target_pairs={{0,2},{1,3},{4,6},{5,7},{8,10},{9,11},{12,14},{13,15},{16,18},{17,... | collective-permute-start | bytes 442376 | tf_op jit(solution)/shard_map/ppermute | solution.py:30
  94.0 19.9 %while.61 = (s32[]{:T(128)}, f32[16,1,3,128]{3,2,1,0:T(4,128)S(1)}, f32[16,1,3,1024]{3,0,2,1:T(8,128)S(1)}, f32[16,1,3,128]{3,2,1,0:T(4,128)S(1)}, f32[16,1,3,1024]{3,0,2,1:T(8,128)S(1)}, /*index=5*/s32[]{:T(128)}) while((s32[]{:T(128)}, f32[16,1,3,128]{3,2,1,0:T(4,128)S(1)}, f32[16,1,3,1024]{3,0,2,1:T(8,128)S(1)}, ...), condition=%wide.region_14.15_spmd, body=%wide.region_11.14_spmd.sunk | while | flops 4587522 | bytes 8560217 | solution.py:104
  114.2 4.2 %collective-permute-start.8 = (f32[4,2,64]{2,1,0:T(2,128)S(1)}, f32[4,2,64]{2,1,0:T(2,128)S(1)}, u32[]{:S(2)}, u32[]{:S(2)}) collective-permute-start(f32[4,2,64]{2,1,0:T(2,128)S(1)} %get-tuple-element.403), channel_id=1, source_target_pairs={{0,4},{4,8},{8,12},{1,5},{5,9},{9,13},{2,6},{6,10},{10,14},{3,7},{... | collective-permute-start | bytes 6152 | tf_op jit(solution)/shard_map/ppermute | solution.py:42
  127.4 4.5 %collective-permute-start.11 = (f32[4,2,18,1]{3,1,0,2:T(2,128)S(1)}, f32[4,2,18,1]{3,1,0,2:T(2,128)S(1)}, u32[]{:S(2)}, u32[]{:S(2)}) collective-permute-start(f32[4,2,18,1]{3,1,0,2:T(2,128)S(1)} %get-tuple-element.396), channel_id=1, source_target_pairs={{0,2},{1,3},{4,6},{5,7},{8,10},{9,11},{12,14},{13,15},{16,18},{17,... | collective-permute-start | bytes 1736 | tf_op jit(solution)/shard_map/ppermute | solution.py:30
  136.7 4.5 %collective-permute-start.13 = (f32[2,1,1,8,6,128]{5,3,0,4,2,1:T(8,128)S(1)}, f32[2,1,1,8,6,128]{5,3,0,4,2,1:T(8,128)S(1)}, u32[]{:S(2)}, u32[]{:S(2)}) collective-permute-start(f32[2,1,1,8,6,128]{5,3,0,4,2,1:T(8,128)S(1)} %maximum_bitcast_fusion.4), channel_id=1, source_target_pairs={{0,4},{4,8},{8,12},{1,5},{5,9},{9,13},{2,6},{6,10},{10,14},{3,7},{... | collective-permute-start | bytes 147464 | tf_op jit(solution)/shard_map/ppermute | solution.py:30
  141.3 5.5 %all_gather.15 = f32[3,512]{1,0:T(4,128)S(1)} all-gather(f32[3,128]{1,0:T(4,128)S(1)} %get-tuple-element.348), channel_id=1, replica_groups=mesh['groups'=2,'age'=4,'span'=2,'blade'=2] {'span','blade'}, dimensions={1}, use_global_device_ids=true | all-gather | bytes 7680 | tf_op jit(solution)/shard_map/all_gather | solution.py:164
  148.3 4.7 %collective-permute-start.15 = (f32[2,3,1,8,6,128]{5,3,0,4,2,1:T(8,128)S(1)}, f32[2,3,1,8,6,128]{5,3,0,4,2,1:T(8,128)S(1)}, u32[]{:S(2)}, u32[]{:S(2)}) collective-permute-start(f32[2,3,1,8,6,128]{5,3,0,4,2,1:T(8,128)S(1)} %pad_maximum_fusion.4), channel_id=1, source_target_pairs={{0,2},{1,3},{4,6},{5,7},{8,10},{9,11},{12,14},{13,15},{16,18},{17,... | collective-permute-start | bytes 442376 | tf_op jit(solution)/shard_map/ppermute | solution.py:30
  153.0 9.9 %while.62 = (s32[]{:T(128)}, f32[16,1,3,128]{3,2,1,0:T(4,128)S(1)}, f32[3,512]{1,0:T(4,128)S(1)}, f32[16,1,3,128]{3,2,1,0:T(4,128)S(1)}, f32[3,512]{1,0:T(4,128)S(1)}, /*index=5*/s32[]{:T(128)}) while((s32[]{:T(128)}, f32[16,1,3,128]{3,2,1,0:T(4,128)S(1)}, f32[3,512]{1,0:T(4,128)S(1)}, f32[16,1,3,128]{3,2,1,0:T(4,128)S(1)}, ...), condition=%wide.region_21.22_spmd, body=%wide.region_17.21_spmd.sunk | while | flops 2293762 | bytes 2133589 | solution.py:104
  164.6 19.9 %while.63 = (s32[]{:T(128)}, f32[16,1,3,128]{3,2,1,0:T(4,128)S(1)}, f32[16,1,3,1024]{3,0,2,1:T(8,128)S(1)}, f32[16,1,3,128]{3,2,1,0:T(4,128)S(1)}, f32[16,1,3,1024]{3,0,2,1:T(8,128)S(1)}, /*index=5*/s32[]{:T(128)}) while((s32[]{:T(128)}, f32[16,1,3,128]{3,2,1,0:T(4,128)S(1)}, f32[16,1,3,1024]{3,0,2,1:T(8,128)S(1)}, ...), condition=%wide.region_25.26_spmd, body=%wide.region_22.25_spmd.sunk | while | flops 4587522 | bytes 8560217 | solution.py:104
  191.6 4.2 %collective-permute-done.19 = f32[4,2,1,64]{3,1,2,0:T(2,128)S(1)} collective-permute-done((f32[4,2,1,64]{3,1,2,0:T(2,128)S(1)}, f32[4,2,1,64]{3,1,2,0:T(2,128)S(1)}, u32[]{:S(2)}, u32[]{:S(2)}) %collective-permute-start.19) | collective-permute-done | bytes 2080 | tf_op jit(solution)/shard_map/ppermute | solution.py:32
  197.3 4.5 %collective-permute-start.20 = (f32[4,2,18,1]{3,1,2,0:T(2,128)S(1)}, f32[4,2,18,1]{3,1,2,0:T(2,128)S(1)}, u32[]{:S(2)}, u32[]{:S(2)}) collective-permute-start(f32[4,2,18,1]{3,1,2,0:T(2,128)S(1)} %get-tuple-element.394), channel_id=1, source_target_pairs={{0,2},{1,3},{4,6},{5,7},{8,10},{9,11},{12,14},{13,15},{16,18},{17,... | collective-permute-start | bytes 1736 | tf_op jit(solution)/shard_map/ppermute | solution.py:30
  206.6 4.5 %collective-permute-start.22 = (f32[2,1,1,8,6,128]{5,3,0,4,2,1:T(8,128)S(1)}, f32[2,1,1,8,6,128]{5,3,0,4,2,1:T(8,128)S(1)}, u32[]{:S(2)}, u32[]{:S(2)}) collective-permute-start(f32[2,1,1,8,6,128]{5,3,0,4,2,1:T(8,128)S(1)} %maximum_bitcast_fusion.5), channel_id=1, source_target_pairs={{0,4},{4,8},{8,12},{1,5},{5,9},{9,13},{2,6},{6,10},{10,14},{3,7},{... | collective-permute-start | bytes 147464 | tf_op jit(solution)/shard_map/ppermute | solution.py:30
  214.2 4.6 %collective-permute-start.24 = (f32[2,3,1,8,6,128]{5,3,0,4,2,1:T(8,128)S(1)}, f32[2,3,1,8,6,128]{5,3,0,4,2,1:T(8,128)S(1)}, u32[]{:S(2)}, u32[]{:S(2)}) collective-permute-start(f32[2,3,1,8,6,128]{5,3,0,4,2,1:T(8,128)S(1)} %pad_maximum_fusion.5), channel_id=1, source_target_pairs={{0,2},{1,3},{4,6},{5,7},{8,10},{9,11},{12,14},{13,15},{16,18},{17,... | collective-permute-start | bytes 442376 | tf_op jit(solution)/shard_map/ppermute | solution.py:30
  218.7 9.9 %while.64 = (s32[]{:T(128)}, f32[16,1,3,128]{3,2,1,0:T(4,128)S(1)}, f32[3,512]{1,0:T(4,128)S(1)}, f32[16,1,3,128]{3,2,1,0:T(4,128)S(1)}, f32[3,512]{1,0:T(4,128)S(1)}, /*index=5*/s32[]{:T(128)}) while((s32[]{:T(128)}, f32[16,1,3,128]{3,2,1,0:T(4,128)S(1)}, f32[3,512]{1,0:T(4,128)S(1)}, f32[16,1,3,128]{3,2,1,0:T(4,128)S(1)}, ...), condition=%wide.region_32.33_spmd, body=%wide.region_28.32_spmd.sunk | while | flops 2293762 | bytes 2133589 | solution.py:104
  230.2 19.9 %while.65 = (s32[]{:T(128)}, f32[16,1,3,128]{3,2,1,0:T(4,128)S(1)}, f32[16,1,3,1024]{3,0,2,1:T(8,128)S(1)}, f32[16,1,3,128]{3,2,1,0:T(4,128)S(1)}, f32[16,1,3,1024]{3,0,2,1:T(8,128)S(1)}, /*index=5*/s32[]{:T(128)}) while((s32[]{:T(128)}, f32[16,1,3,128]{3,2,1,0:T(4,128)S(1)}, f32[16,1,3,1024]{3,0,2,1:T(8,128)S(1)}, ...), condition=%wide.region_36.37_spmd, body=%wide.region_33.36_spmd.sunk | while | flops 4587522 | bytes 8560217 | solution.py:104
  250.4 4.2 %collective-permute-start.26 = (f32[4,2,64]{2,1,0:T(2,128)S(1)}, f32[4,2,64]{2,1,0:T(2,128)S(1)}, u32[]{:S(2)}, u32[]{:S(2)}) collective-permute-start(f32[4,2,64]{2,1,0:T(2,128)S(1)} %bitcast.385), channel_id=1, source_target_pairs={{0,4},{4,8},{8,12},{1,5},{5,9},{9,13},{2,6},{6,10},{10,14},{3,7},{... | collective-permute-start | bytes 6152 | tf_op jit(solution)/shard_map/ppermute | solution.py:42
  (981 shorter events, 146.3 us)
Async XLA Ops:
  2.7 64.2 %collective-permute-start = (f32[4,2,1,64]{3,1,2,0:T(2,128)S(1)}, f32[4,2,1,64]{3,1,2,0:T(2,128)S(1)}, u32[]{:S(2)}, u32[]{:S(2)}) collective-permute-start(f32[4,2,1,64]{3,1,2,0:T(2,128)S(1)} %copy.303), channel_id=1, source_target_pairs={{0,4},{4,8},{8,12},{1,5},{5,9},{9,13},{2,6},{6,10},{10,14},{3,7},{... | collective-permute-start | bytes 6152 | tf_op jit(solution)/shard_map/ppermute | solution.py:30
  7.7 59.3 %collective-permute-start.1 = (f32[4,2,1,64]{3,1,2,0:T(2,128)S(1)}, f32[4,2,1,64]{3,1,2,0:T(2,128)S(1)}, u32[]{:S(2)}, u32[]{:S(2)}) collective-permute-start(f32[4,2,1,64]{3,1,2,0:T(2,128)S(1)} %copy.304), channel_id=1, source_target_pairs={{4,0},{8,4},{12,8},{5,1},{9,5},{13,9},{6,2},{10,6},{14,10},{7,3},{... | collective-permute-start | bytes 6152 | tf_op jit(solution)/shard_map/ppermute | solution.py:32
  67.2 6.4 %collective-permute-start.3 = (f32[4,2,18,1]{3,1,2,0:T(2,128)S(1)}, f32[4,2,18,1]{3,1,2,0:T(2,128)S(1)}, u32[]{:S(2)}, u32[]{:S(2)}) collective-permute-start(f32[4,2,18,1]{3,1,2,0:T(2,128)S(1)} %get-tuple-element.399), channel_id=1, source_target_pairs={{2,0},{3,1},{6,4},{7,5},{10,8},{11,9},{14,12},{15,13},{18,16},{19,... | collective-permute-start | bytes 1736 | tf_op jit(solution)/shard_map/ppermute | solution.py:32
  68.5 6.5 %collective-permute-start.2 = (f32[4,2,18,1]{3,1,2,0:T(2,128)S(1)}, f32[4,2,18,1]{3,1,2,0:T(2,128)S(1)}, u32[]{:S(2)}, u32[]{:S(2)}) collective-permute-start(f32[4,2,18,1]{3,1,2,0:T(2,128)S(1)} %get-tuple-element.398), channel_id=1, source_target_pairs={{0,2},{1,3},{4,6},{5,7},{8,10},{9,11},{12,14},{13,15},{16,18},{17,... | collective-permute-start | bytes 1736 | tf_op jit(solution)/shard_map/ppermute | solution.py:30
  76.4 6.0 %collective-permute-start.5 = (f32[2,1,1,8,6,128]{5,3,0,4,2,1:T(8,128)S(1)}, f32[2,1,1,8,6,128]{5,3,0,4,2,1:T(8,128)S(1)}, u32[]{:S(2)}, u32[]{:S(2)}) collective-permute-start(f32[2,1,1,8,6,128]{5,3,0,4,2,1:T(8,128)S(1)} %maximum_bitcast_fusion.3), channel_id=1, source_target_pairs={{4,0},{8,4},{12,8},{5,1},{9,5},{13,9},{6,2},{10,6},{14,10},{7,3},{... | collective-permute-start | bytes 147464 | tf_op jit(solution)/shard_map/ppermute | solution.py:32
  77.7 6.3 %collective-permute-start.4 = (f32[2,1,1,8,6,128]{5,3,0,4,2,1:T(8,128)S(1)}, f32[2,1,1,8,6,128]{5,3,0,4,2,1:T(8,128)S(1)}, u32[]{:S(2)}, u32[]{:S(2)}) collective-permute-start(f32[2,1,1,8,6,128]{5,3,0,4,2,1:T(8,128)S(1)} %maximum_bitcast_fusion.3), channel_id=1, source_target_pairs={{0,4},{4,8},{8,12},{1,5},{5,9},{9,13},{2,6},{6,10},{10,14},{3,7},{... | collective-permute-start | bytes 147464 | tf_op jit(solution)/shard_map/ppermute | solution.py:30
  84.0 7.0 %collective-permute-start.7 = (f32[2,3,1,8,6,128]{5,3,0,4,2,1:T(8,128)S(1)}, f32[2,3,1,8,6,128]{5,3,0,4,2,1:T(8,128)S(1)}, u32[]{:S(2)}, u32[]{:S(2)}) collective-permute-start(f32[2,3,1,8,6,128]{5,3,0,4,2,1:T(8,128)S(1)} %pad_maximum_fusion.3), channel_id=1, source_target_pairs={{2,0},{3,1},{6,4},{7,5},{10,8},{11,9},{14,12},{15,13},{18,16},{19,... | collective-permute-start | bytes 442376 | tf_op jit(solution)/shard_map/ppermute | solution.py:32
  85.3 7.2 %collective-permute-start.6 = (f32[2,3,1,8,6,128]{5,3,0,4,2,1:T(8,128)S(1)}, f32[2,3,1,8,6,128]{5,3,0,4,2,1:T(8,128)S(1)}, u32[]{:S(2)}, u32[]{:S(2)}) collective-permute-start(f32[2,3,1,8,6,128]{5,3,0,4,2,1:T(8,128)S(1)} %pad_maximum_fusion.3), channel_id=1, source_target_pairs={{0,2},{1,3},{4,6},{5,7},{8,10},{9,11},{12,14},{13,15},{16,18},{17,... | collective-permute-start | bytes 442376 | tf_op jit(solution)/shard_map/ppermute | solution.py:30
  114.2 6.3 %collective-permute-start.8 = (f32[4,2,64]{2,1,0:T(2,128)S(1)}, f32[4,2,64]{2,1,0:T(2,128)S(1)}, u32[]{:S(2)}, u32[]{:S(2)}) collective-permute-start(f32[4,2,64]{2,1,0:T(2,128)S(1)} %get-tuple-element.403), channel_id=1, source_target_pairs={{0,4},{4,8},{8,12},{1,5},{5,9},{9,13},{2,6},{6,10},{10,14},{3,7},{... | collective-permute-start | bytes 6152 | tf_op jit(solution)/shard_map/ppermute | solution.py:42
  120.5 5.5 %collective-permute-start.10 = (f32[4,2,1,64]{3,1,0,2:T(2,128)S(1)}, f32[4,2,1,64]{3,1,0,2:T(2,128)S(1)}, u32[]{:S(2)}, u32[]{:S(2)}) collective-permute-start(f32[4,2,1,64]{3,1,0,2:T(2,128)S(1)} %fusion.57), channel_id=1, source_target_pairs={{4,0},{8,4},{12,8},{5,1},{9,5},{13,9},{6,2},{10,6},{14,10},{7,3},{... | collective-permute-start | bytes 6152 | tf_op jit(solution)/shard_map/ppermute | solution.py:32
  126.1 6.2 %collective-permute-start.12 = (f32[4,2,18,1]{3,1,0,2:T(2,128)S(1)}, f32[4,2,18,1]{3,1,0,2:T(2,128)S(1)}, u32[]{:S(2)}, u32[]{:S(2)}) collective-permute-start(f32[4,2,18,1]{3,1,0,2:T(2,128)S(1)} %get-tuple-element.397), channel_id=1, source_target_pairs={{2,0},{3,1},{6,4},{7,5},{10,8},{11,9},{14,12},{15,13},{18,16},{19,... | collective-permute-start | bytes 1736 | tf_op jit(solution)/shard_map/ppermute | solution.py:32
  127.4 6.5 %collective-permute-start.11 = (f32[4,2,18,1]{3,1,0,2:T(2,128)S(1)}, f32[4,2,18,1]{3,1,0,2:T(2,128)S(1)}, u32[]{:S(2)}, u32[]{:S(2)}) collective-permute-start(f32[4,2,18,1]{3,1,0,2:T(2,128)S(1)} %get-tuple-element.396), channel_id=1, source_target_pairs={{0,2},{1,3},{4,6},{5,7},{8,10},{9,11},{12,14},{13,15},{16,18},{17,... | collective-permute-start | bytes 1736 | tf_op jit(solution)/shard_map/ppermute | solution.py:30
  135.4 11.5 %collective-permute-start.14 = (f32[2,1,1,8,6,128]{5,3,0,4,2,1:T(8,128)S(1)}, f32[2,1,1,8,6,128]{5,3,0,4,2,1:T(8,128)S(1)}, u32[]{:S(2)}, u32[]{:S(2)}) collective-permute-start(f32[2,1,1,8,6,128]{5,3,0,4,2,1:T(8,128)S(1)} %maximum_bitcast_fusion.4), channel_id=1, source_target_pairs={{4,0},{8,4},{12,8},{5,1},{9,5},{13,9},{6,2},{10,6},{14,10},{7,3},{... | collective-permute-start | bytes 147464 | tf_op jit(solution)/shard_map/ppermute | solution.py:32
  136.7 10.2 %collective-permute-start.13 = (f32[2,1,1,8,6,128]{5,3,0,4,2,1:T(8,128)S(1)}, f32[2,1,1,8,6,128]{5,3,0,4,2,1:T(8,128)S(1)}, u32[]{:S(2)}, u32[]{:S(2)}) collective-permute-start(f32[2,1,1,8,6,128]{5,3,0,4,2,1:T(8,128)S(1)} %maximum_bitcast_fusion.4), channel_id=1, source_target_pairs={{0,4},{4,8},{8,12},{1,5},{5,9},{9,13},{2,6},{6,10},{10,14},{3,7},{... | collective-permute-start | bytes 147464 | tf_op jit(solution)/shard_map/ppermute | solution.py:30
  147.0 16.1 %collective-permute-start.16 = (f32[2,3,1,8,6,128]{5,3,0,4,2,1:T(8,128)S(1)}, f32[2,3,1,8,6,128]{5,3,0,4,2,1:T(8,128)S(1)}, u32[]{:S(2)}, u32[]{:S(2)}) collective-permute-start(f32[2,3,1,8,6,128]{5,3,0,4,2,1:T(8,128)S(1)} %pad_maximum_fusion.4), channel_id=1, source_target_pairs={{2,0},{3,1},{6,4},{7,5},{10,8},{11,9},{14,12},{15,13},{18,16},{19,... | collective-permute-start | bytes 442376 | tf_op jit(solution)/shard_map/ppermute | solution.py:32
  148.3 14.8 %collective-permute-start.15 = (f32[2,3,1,8,6,128]{5,3,0,4,2,1:T(8,128)S(1)}, f32[2,3,1,8,6,128]{5,3,0,4,2,1:T(8,128)S(1)}, u32[]{:S(2)}, u32[]{:S(2)}) collective-permute-start(f32[2,3,1,8,6,128]{5,3,0,4,2,1:T(8,128)S(1)} %pad_maximum_fusion.4), channel_id=1, source_target_pairs={{0,2},{1,3},{4,6},{5,7},{8,10},{9,11},{12,14},{13,15},{16,18},{17,... | collective-permute-start | bytes 442376 | tf_op jit(solution)/shard_map/ppermute | solution.py:30
  184.8 5.5 %collective-permute-start.17 = (f32[4,2,64]{2,1,0:T(2,128)S(1)}, f32[4,2,64]{2,1,0:T(2,128)S(1)}, u32[]{:S(2)}, u32[]{:S(2)}) collective-permute-start(f32[4,2,64]{2,1,0:T(2,128)S(1)} %get-tuple-element.401), channel_id=1, source_target_pairs={{0,4},{4,8},{8,12},{1,5},{5,9},{9,13},{2,6},{6,10},{10,14},{3,7},{... | collective-permute-start | bytes 6152 | tf_op jit(solution)/shard_map/ppermute | solution.py:42
  196.0 6.2 %collective-permute-start.21 = (f32[4,2,18,1]{3,1,2,0:T(2,128)S(1)}, f32[4,2,18,1]{3,1,2,0:T(2,128)S(1)}, u32[]{:S(2)}, u32[]{:S(2)}) collective-permute-start(f32[4,2,18,1]{3,1,2,0:T(2,128)S(1)} %get-tuple-element.395), channel_id=1, source_target_pairs={{2,0},{3,1},{6,4},{7,5},{10,8},{11,9},{14,12},{15,13},{18,16},{19,... | collective-permute-start | bytes 1736 | tf_op jit(solution)/shard_map/ppermute | solution.py:32
  197.3 6.5 %collective-permute-start.20 = (f32[4,2,18,1]{3,1,2,0:T(2,128)S(1)}, f32[4,2,18,1]{3,1,2,0:T(2,128)S(1)}, u32[]{:S(2)}, u32[]{:S(2)}) collective-permute-start(f32[4,2,18,1]{3,1,2,0:T(2,128)S(1)} %get-tuple-element.394), channel_id=1, source_target_pairs={{0,2},{1,3},{4,6},{5,7},{8,10},{9,11},{12,14},{13,15},{16,18},{17,... | collective-permute-start | bytes 1736 | tf_op jit(solution)/shard_map/ppermute | solution.py:30
  205.3 6.0 %collective-permute-start.23 = (f32[2,1,1,8,6,128]{5,3,0,4,2,1:T(8,128)S(1)}, f32[2,1,1,8,6,128]{5,3,0,4,2,1:T(8,128)S(1)}, u32[]{:S(2)}, u32[]{:S(2)}) collective-permute-start(f32[2,1,1,8,6,128]{5,3,0,4,2,1:T(8,128)S(1)} %maximum_bitcast_fusion.5), channel_id=1, source_target_pairs={{4,0},{8,4},{12,8},{5,1},{9,5},{13,9},{6,2},{10,6},{14,10},{7,3},{... | collective-permute-start | bytes 147464 | tf_op jit(solution)/shard_map/ppermute | solution.py:32
  206.6 6.3 %collective-permute-start.22 = (f32[2,1,1,8,6,128]{5,3,0,4,2,1:T(8,128)S(1)}, f32[2,1,1,8,6,128]{5,3,0,4,2,1:T(8,128)S(1)}, u32[]{:S(2)}, u32[]{:S(2)}) collective-permute-start(f32[2,1,1,8,6,128]{5,3,0,4,2,1:T(8,128)S(1)} %maximum_bitcast_fusion.5), channel_id=1, source_target_pairs={{0,4},{4,8},{8,12},{1,5},{5,9},{9,13},{2,6},{6,10},{10,14},{3,7},{... | collective-permute-start | bytes 147464 | tf_op jit(solution)/shard_map/ppermute | solution.py:30
  212.9 15.9 %collective-permute-start.25 = (f32[2,3,1,8,6,128]{5,3,0,4,2,1:T(8,128)S(1)}, f32[2,3,1,8,6,128]{5,3,0,4,2,1:T(8,128)S(1)}, u32[]{:S(2)}, u32[]{:S(2)}) collective-permute-start(f32[2,3,1,8,6,128]{5,3,0,4,2,1:T(8,128)S(1)} %pad_maximum_fusion.5), channel_id=1, source_target_pairs={{2,0},{3,1},{6,4},{7,5},{10,8},{11,9},{14,12},{15,13},{18,16},{19,... | collective-permute-start | bytes 442376 | tf_op jit(solution)/shard_map/ppermute | solution.py:32
  214.2 14.6 %collective-permute-start.24 = (f32[2,3,1,8,6,128]{5,3,0,4,2,1:T(8,128)S(1)}, f32[2,3,1,8,6,128]{5,3,0,4,2,1:T(8,128)S(1)}, u32[]{:S(2)}, u32[]{:S(2)}) collective-permute-start(f32[2,3,1,8,6,128]{5,3,0,4,2,1:T(8,128)S(1)} %pad_maximum_fusion.5), channel_id=1, source_target_pairs={{0,2},{1,3},{4,6},{5,7},{8,10},{9,11},{12,14},{13,15},{16,18},{17,... | collective-permute-start | bytes 442376 | tf_op jit(solution)/shard_map/ppermute | solution.py:30
  250.4 5.6 %collective-permute-start.26 = (f32[4,2,64]{2,1,0:T(2,128)S(1)}, f32[4,2,64]{2,1,0:T(2,128)S(1)}, u32[]{:S(2)}, u32[]{:S(2)}) collective-permute-start(f32[4,2,64]{2,1,0:T(2,128)S(1)} %bitcast.385), channel_id=1, source_target_pairs={{0,4},{4,8},{8,12},{1,5},{5,9},{9,13},{2,6},{6,10},{10,14},{3,7},{... | collective-permute-start | bytes 6152 | tf_op jit(solution)/shard_map/ppermute | solution.py:42
  (6 other events, 75.8 us)
where the time goes:
time: 258 us; the launch traced here: 257 us
  other arithmetic  91.1 us (35%)
  starting transfers between devices  77.3 us (30%)
  blocking collectives  34.4 us (13%)
  waiting for transfers between devices  20.1 us (8%)
  local copies, waits for them, and re-layouts  16.5 us (6%)
  between operations  11.3 us (4%)
  loops' own time  5.87 us (2%)
    ppermute x12, starting transfers between devices, with_halo(): lax.ppermute(tail, axis, [(i, (i + 1) % count) for i in range(ends)])  49.9 us
    all_gather x3, blocking collectives, on_device(): lax.all_gather(moment_got, ('span', 'blade'), axis=1, tiled=True)  15.9 us
    ppermute x12, starting transfers between devices, with_halo(): lax.ppermute(head, axis, [((i + 1) % count, i) for i in range(ends)])  15.5 us
    sub x48, other arithmetic, near_velocity(): strengths[1][None, :] * separation[2]  14.4 us
    reduce_sum x48, other arithmetic, far_velocity(): return inv_four_pi * jnp.sum(values, axis=2)  13.4 us
    psum x1, blocking collectives, spread(): return lax.psum(jnp.where(mine, shard, jnp.zeros_like(shard)), axis)  13.3 us
    ppermute x3, starting transfers between devices, shifted(): lax.ppermute(value, axis, [(source, source + steps) for source in range(f...  11.9 us
    reduce_sum x48, other arithmetic, near_velocity(): dist_sq = jnp.sum(separation * separation, axis=0) + near_core  10.6 us
  transfers between devices with their start and end apart: 27, of which 14 were waited for; matrix products, arithmetic and copies ran while one was open for 15% of the time, Pallas kernels for 0%

commit v1 on v0

v1 whole, which is shorter than its diff:
```python
import functools
import math

import jax
import jax.numpy as jnp
from jax import lax
from jax.experimental import pallas as pl
from jax.experimental.pallas import tpu as pltpu
from jax.sharding import PartitionSpec as P

CB = 8
STEP = 0.05
NEAR_CORE = 0.0025
FAR_CORE = 0.01
INV_FOUR_PI = 0.25 / math.pi
MESH = pl.DeviceIdType.MESH
HIGH = lax.Precision.HIGHEST
F32 = jnp.float32


def dot(a, b):
    return jnp.dot(a, b, preferred_element_type=F32, precision=HIGH)


def wake_kernel(
    sizes,
    az_ref, fs_ref, src_ref, tgt_ref,
    hot_ref, mu_ref, cen_ref, nrm_ref, te_ref, state_ref,
    final_ref, vel_ref,
    g1, g2, srcs, cur, moved, tile_out, shed, tail_in, side_in, far_out, near_out,
    g1_send, g1_recv, g2_send, g2_recv, a_send, a_recv, b_send, b_recv, *tables,
):
    n_age, n_span, n_blade, steps, az_dev = sizes
    entries = near_out.shape[1]
    age = lax.axis_index("age")
    span = lax.axis_index("span")
    blade = lax.axis_index("blade")
    n_plane = n_span * n_blade
    place = span * n_blade + blade
    naz = az_dev * n_age
    nb = 2 * n_blade
    first_age = age == 0
    last_age = age == n_age - 1

    for table in tables:
        table[...] = jnp.zeros_like(table)

    around = [(da, ds) for da in (-1, 0, 1) for ds in (-1, 0, 1) if (da, ds) != (0, 0)]

    def exists(da, ds):
        ok = jnp.bool_(True)
        if da < 0:
            ok = age > 0
        if da > 0:
            ok = age < n_age - 1
        if ds < 0:
            ok = jnp.logical_and(ok, span > 0)
        if ds > 0:
            ok = jnp.logical_and(ok, span < n_span - 1)
        return ok

    def spot(da, ds):
        return {"age": age + da, "span": span + ds, "blade": blade}

    def age_peer(off):
        return lax.rem(age + off, n_age)

    def plane_peer(off):
        other = lax.rem(place + off, n_plane)
        return other, {"age": age, "span": other // n_blade, "blade": lax.rem(other, n_blade)}

    diagonals = [(da, ds) for da, ds in around if da and ds]
    barrier = pltpu.get_barrier_semaphore()
    for off in range(1, n_age):
        pl.semaphore_signal(
            barrier, inc=1, device_id={"age": age_peer(off), "span": span, "blade": blade}, device_id_type=MESH
        )
    for off in range(1, n_plane):
        pl.semaphore_signal(barrier, inc=1, device_id=plane_peer(off)[1], device_id_type=MESH)
    for da, ds in diagonals:
        @pl.when(exists(da, ds))
        def _(da=da, ds=ds):
            pl.semaphore_signal(barrier, inc=1, device_id=spot(da, ds), device_id_type=MESH)

    lane8 = lax.broadcasted_iota(jnp.int32, (8, 128), 1)
    sub8 = lax.broadcasted_iota(jnp.int32, (8, 128), 0)
    low = lane8 < 64
    lane1 = lax.broadcasted_iota(jnp.int32, (1, 128), 1)
    low1 = lane1 < 64

    turn = jnp.zeros((8, 128), F32)
    for k in range(steps):
        turn = jnp.where(sub8 == k, az_ref[k].astype(F32) / naz, turn)
    frac = (blade * 2 + lane8 // 64).astype(F32) / nb
    angle = 2.0 * math.pi * (turn + frac)
    cosine = jnp.cos(angle)
    sine = jnp.sin(angle)

    def turned(k, x, y, z):
        c = cosine[k:k + 1]
        s = sine[k:k + 1]
        return x * c - y * s, x * s + y * c, z

    col = lax.broadcasted_iota(jnp.int32, (64, 128), 1)
    row = lax.broadcasted_iota(jnp.int32, (64, 128), 0)
    spread = (row // CB == col % CB).astype(F32)
    place_lane = (row == col % 64).astype(F32)
    col2 = lax.broadcasted_iota(jnp.int32, (128, 128), 1)
    row2 = lax.broadcasted_iota(jnp.int32, (128, 128), 0)
    keep = (row2 // CB == col2 // CB).astype(F32)

    def coarse(values):
        return jnp.sum(dot(values, spread) * keep, axis=0, keepdims=True)

    centers = [coarse(cen_ref[c]) * (1.0 / (CB * CB)) for c in range(3)]
    for k in range(steps):
        az = az_ref[k]
        mine = (az // az_dev == age).astype(F32)
        now = mu_ref[lax.rem(az, az_dev)]
        m = [coarse(now * nrm_ref[c]) * INV_FOUR_PI for c in range(3)]
        rows = list(turned(k, *m)) + list(turned(k, *centers))
        d0 = jnp.broadcast_to(now[63:64] - now[0:1], (8, 64))
        d1 = jnp.broadcast_to(now[127:128] - now[64:65], (8, 64))
        trail = jnp.where(low, dot(d0, place_lane), dot(d1, place_lane))[0:1]
        rows.append(trail)
        for i, value in enumerate(rows):
            g1[age, 8 * k + i:8 * k + i + 1, :] = value * mine
        g1[age, 8 * k + 7:8 * k + 8, :] = jnp.zeros((1, 128), F32)

    cur[...] = state_ref[...]
    for cb in range(8):
        tile_out[0, cb:cb + 1, :] = state_ref[cb, 7:8, :]
        tile_out[steps + 1, cb:cb + 1, :] = state_ref[cb, 0:1, :]

    peers = n_age - 1 + n_plane - 1
    for da, ds in diagonals:
        peers = peers + exists(da, ds).astype(jnp.int32)
    pl.semaphore_wait(barrier, peers)

    def send_g1(off):
        to = age_peer(off)
        return pltpu.make_async_remote_copy(
            g1.at[age], g1.at[age], g1_send.at[off], g1_recv.at[off],
            device_id={"age": to, "span": span, "blade": blade}, device_id_type=MESH)

    def recv_g1(off):
        frm = lax.rem(age - off + n_age, n_age)
        return pltpu.make_async_remote_copy(
            g1.at[age], g1.at[frm], g1_send.at[off], g1_recv.at[off],
            device_id={"age": age_peer(off), "span": span, "blade": blade}, device_id_type=MESH)

    for off in range(1, n_age):
        send_g1(off).start()

    def side_copy(k, src, ds):
        slot = 0 if ds > 0 else 1
        return pltpu.make_async_remote_copy(
            src, side_in.at[k, slot], a_send.at[k, slot], a_recv.at[k, slot],
            device_id=spot(0, ds), device_id_type=MESH)

    def tail_copy(k, src, da, ds, slot, send):
        return pltpu.make_async_remote_copy(
            src, tail_in.at[k, slot], a_send.at[k, send], a_recv.at[k, 2 + slot],
            device_id=spot(da, ds), device_id_type=MESH)

    def edge_plan(k):
        plan = []
        block = cur if k == 0 else moved.at[k - 1]
        if k < steps:
            for ds in (-1, 1):
                plan.append((exists(0, ds), exists(0, -ds), side_copy(k, block, ds)))
        plan.append((exists(1, 0), exists(-1, 0), tail_copy(k, tile_out.at[k], 1, 0, 0, 2)))
        if k == 0:
            plan.append((exists(-1, 0), exists(1, 0), tail_copy(k, tile_out.at[steps + 1], -1, 0, 3, 3)))
        elif k < steps:
            for ds in (-1, 1):
                slot = 1 if ds > 0 else 2
                plan.append((exists(1, ds), exists(-1, -ds), tail_copy(k, tile_out.at[k], 1, ds, slot, 2 + slot)))
                plan.append((
                    jnp.logical_and(first_age, exists(0, ds)), jnp.logical_and(first_age, exists(0, -ds)),
                    tail_copy(k, shed.at[k - 1], 0, ds, slot, 4 + slot)))
        return plan

    def start(plan):
        for out, _, copy in plan:
            pl.when(out)(copy.start)

    def finish(plan):
        for _, come, copy in plan:
            pl.when(come)(copy.wait_recv)
        for out, _, copy in plan:
            pl.when(out)(copy.wait_send)

    def block_plan(k):
        plan = []
        for da, ds in around:
            slot = (1 - da) * 3 + 1 - ds
            copy = pltpu.make_async_remote_copy(
                tables[k].at[pl.ds(64, 16)], tables[k].at[pl.ds(slot * 16, 16)],
                b_send.at[k, slot], b_recv.at[k, slot], device_id=spot(da, ds), device_id_type=MESH)
            plan.append((exists(da, ds), exists(-da, -ds), copy))
        return plan

    def roll64(v):
        return pltpu.roll(v, 64, 1)

    def down(v):
        return pltpu.roll(v, 1, 0)

    def aged(block, tail):
        r = roll64(block)
        first = jnp.broadcast_to(roll64(tail), (8, 128))
        return jnp.where(low, jnp.where(sub8 == 0, first, down(r)), r)

    def strengths(k):
        for b in range(2):
            diff = []
            for c in range(4):
                cb = 2 * c + b
                v = cur[cb]
                r = roll64(v)
                own_pos = c < 3
                above_edge = v[0:1] if own_pos else jnp.zeros((1, 128), F32)
                below_edge = v[7:8] if own_pos else jnp.zeros((1, 128), F32)
                tail = tail_in[k, 0, cb:cb + 1, :]
                if k == 0:
                    up_row = jnp.where(first_age, above_edge, roll64(tail))
                    head = tail_in[k, 3, cb:cb + 1, :]
                    down_row = jnp.where(last_age, below_edge, roll64(head))
                else:
                    up_row = jnp.where(first_age, above_edge, tail)
                    down_row = jnp.where(last_age, below_edge, moved[k - 1, cb, 7:8, :])
                before = jnp.where(low, jnp.where(sub8 == 0, jnp.broadcast_to(up_row, (8, 128)), down(r)), r)
                after = jnp.where(
                    low, r, jnp.where(sub8 == 7, jnp.broadcast_to(down_row, (8, 128)), pltpu.roll(r, 7, 0)))
                edge = v if own_pos else jnp.zeros((8, 128), F32)
                left, right = side_in[k, 0, cb], side_in[k, 1, cb]
                if k > 0:
                    left = aged(left, tail_in[k, 1, cb:cb + 1, :])
                    right = aged(right, tail_in[k, 2, cb:cb + 1, :])
                left = jnp.where(span == 0, edge, pltpu.roll(left, 65, 1))
                right = jnp.where(span == n_span - 1, edge, pltpu.roll(right, 63, 1))
                minus = jnp.where(lane8 % 64 == 0, left, pltpu.roll(v, 1, 1))
                plus = jnp.where(lane8 % 64 == 63, right, pltpu.roll(v, 127, 1))
                diff.append((0.5 * (after - before), 0.5 * (plus - minus)))
                if own_pos:
                    for t in range(8):
                        tables[k][64 + b * 8 + t, c:c + 1, :] = v[t:t + 1]
            mu_r, mu_s = diff[3]
            for c in range(3):
                value = (mu_s * diff[c][0] - mu_r * diff[c][1]) * INV_FOUR_PI
                for t in range(8):
                    tables[k][64 + b * 8 + t, 3 + c:4 + c, :] = value[t:t + 1]

    groups = srcs.shape[1] // 8

    def fill_sources(k):
        for p in range(n_plane):
            cols = jnp.transpose(g2[p, 8 * k:8 * k + 8, :])
            for i in range(6):
                srcs[i, 128 * p:128 * p + 128, :] = jnp.broadcast_to(cols[:, i:i + 1], (128, 128))

    def far(t0):
        def per_blade(b, carry):
            goal = [
                [jnp.broadcast_to(cur[2 * c + b, t0 + i:t0 + i + 1, :], (8, 128)) for c in range(3)]
                for i in range(4)
            ]

            def body(g, acc):
                at = pl.ds(pl.multiple_of(g * 8, 8), 8)
                cx, cy, cz = srcs[3, at, :], srcs[4, at, :], srcs[5, at, :]
                mx, my, mz = srcs[0, at, :], srcs[1, at, :], srcs[2, at, :]
                out = []
                for i in range(4):
                    dx, dy, dz = goal[i][0] - cx, goal[i][1] - cy, goal[i][2] - cz
                    r = lax.rsqrt(dx * dx + dy * dy + (dz * dz + FAR_CORE))
                    r2 = r * r
                    r3 = r2 * r
                    t = (mx * dx + my * dy + mz * dz) * (3.0 * r2)
                    out.append(acc[3 * i] + r3 * (t * dx - mx))
                    out.append(acc[3 * i + 1] + r3 * (t * dy - my))
                    out.append(acc[3 * i + 2] + r3 * (t * dz - mz))
                return tuple(out)

            acc = lax.fori_loop(0, groups, body, tuple(jnp.zeros((8, 128), F32) for _ in range(12)))
            for i in range(4):
                for c in range(3):
                    far_out[2 * c + b, t0 + i:t0 + i + 1, :] = jnp.sum(acc[3 * i + c], axis=0, keepdims=True)
            return carry

        lax.fori_loop(0, 2, per_blade, 0)

    def near(k):
        def body(e, carry):
            s = src_ref[e]
            t = tgt_ref[e]
            cols = jnp.transpose(tables[k][s])
            goal_tile = tables[k][64 + t]
            goal = [jnp.broadcast_to(goal_tile[c:c + 1], (8, 128)) for c in range(3)]
            acc = [jnp.zeros((8, 128), F32) for _ in range(3)]
            for g in range(16):
                part = cols[8 * g:8 * g + 8, :]
                px, py, pz, sx, sy, sz = [jnp.broadcast_to(part[:, i:i + 1], (8, 128)) for i in range(6)]
                dx, dy, dz = goal[0] - px, goal[1] - py, goal[2] - pz
                r = lax.rsqrt(dx * dx + dy * dy + (dz * dz + NEAR_CORE))
                w = r * r * r
                acc[0] += w * (sy * dz - sz * dy)
                acc[1] += w * (sz * dx - sx * dz)
                acc[2] += w * (sx * dy - sy * dx)
            for c in range(3):
                near_out[c, pl.ds(e, 1), :] = jnp.sum(acc[c], axis=0, keepdims=True)
            return carry

        lax.fori_loop(0, entries, body, 0)

    plan = edge_plan(0)
    start(plan)
    finish(plan)
    strengths(0)
    blocks = block_plan(0)
    start(blocks)

    for off in range(1, n_age):
        recv_g1(off).wait_recv()
    total = g1[0]
    for i in range(1, n_age):
        total = total + g1[i]
    g2[place] = total

    def send_g2(off):
        return pltpu.make_async_remote_copy(
            g2.at[place], g2.at[place], g2_send.at[off], g2_recv.at[off],
            device_id=plane_peer(off)[1], device_id_type=MESH)

    def recv_g2(off):
        frm = lax.rem(place - off + n_plane, n_plane)
        return pltpu.make_async_remote_copy(
            g2.at[place], g2.at[frm], g2_send.at[off], g2_recv.at[off],
            device_id=plane_peer(off)[1], device_id_type=MESH)

    for off in range(1, n_plane):
        send_g2(off).start()

    for k in range(steps):
        te = turned(k, te_ref[0:1], te_ref[1:2], te_ref[2:3])
        lines = list(te) + [total[8 * k + 6:8 * k + 7]]
        for c in range(4):
            flipped = roll64(lines[c])
            beyond = (lines[c], flipped) if c < 3 else (jnp.zeros((1, 128), F32),) * 2
            shed[k, 2 * c:2 * c + 1, :] = jnp.where(low1, beyond[0], flipped)
            shed[k, 2 * c + 1:2 * c + 2, :] = jnp.where(low1, beyond[1], lines[c])

    for off in range(1, n_plane):
        recv_g2(off).wait_recv()
    for off in range(1, n_age):
        send_g1(off).wait_send()
    for off in range(1, n_plane):
        send_g2(off).wait_send()

    def incoming(k, cb):
        return jnp.where(first_age, shed[k - 1, cb:cb + 1, :], tail_in[k, 0, cb:cb + 1, :])

    for k in range(steps):
        fill_sources(k)
        far(4)
        if k > 0:
            finish(plan)
            for cb in range(8):
                cur[cb] = aged(moved[k - 1, cb], incoming(k, cb))
            strengths(k)
            blocks = block_plan(k)
            start(blocks)
        far(0)
        finish(blocks)
        near(k)
        hot = hot_ref[...]
        for c in range(3):
            close = dot(hot, near_out[c])
            for b in range(2):
                v = fs_ref[c] + far_out[2 * c + b] + close[8 * b:8 * b + 8]
                if k == steps - 1:
                    vel_ref[2 * c + b] = v
                moved[k, 2 * c + b] = cur[2 * c + b] + STEP * v
        for b in range(2):
            moved[k, 6 + b] = cur[6 + b]
        for cb in range(8):
            tile_out[k + 1, cb:cb + 1, :] = moved[k, cb, 7:8, :]
        plan = edge_plan(k + 1)
        start(plan)
        if k < steps - 1:
            for cb in range(8):
                cur[cb] = aged(moved[k, cb], shed[k, cb:cb + 1, :])
    finish(plan)
    for cb in range(8):
        final_ref[cb] = aged(moved[steps - 1, cb], incoming(steps, cb))


def on_device(
    surface_mu, centroid_body, area_normal, te_body, wake_state, pairs, az_index, free_stream
):
    az_dev = surface_mu.shape[0]
    blades, tiles = wake_state.shape[1:3]
    steps = az_index.shape[0]
    slots = pairs.shape[3]
    n_age, n_span, n_blade = (lax.axis_size(a) for a in ("age", "span", "blade"))
    n_plane = n_span * n_blade
    count = blades * tiles * slots
    entries = count // 2

    ids = pairs.reshape(count)
    live = ids >= 0
    order = jnp.arange(count, dtype=jnp.int32)
    rank = jnp.sum((live[None, :] & (order[None, :] < order[:, None])).astype(jnp.int32), axis=1)
    chosen = live[None, :] & (rank[None, :] == jnp.arange(entries, dtype=jnp.int32)[:, None])
    place = (ids // 8) * (blades * tiles) + order // (tiles * slots) * tiles + ids % 8
    empty = 9 * blades * tiles
    src = empty + jnp.sum(jnp.where(chosen, place[None, :] - empty, 0), axis=1)
    tgt = jnp.sum(jnp.where(chosen, order[None, :] // slots, 0), axis=1)
    hot = (tgt[None, :] == jnp.arange(blades * tiles, dtype=jnp.int32)[:, None]).astype(F32)

    vm = pl.BlockSpec(memory_space=pltpu.VMEM)
    sm = pl.BlockSpec(memory_space=pltpu.SMEM)
    dma = pltpu.SemaphoreType.DMA
    final, vel = pl.pallas_call(
        functools.partial(wake_kernel, (n_age, n_span, n_blade, steps, az_dev)),
        out_shape=(
            jax.ShapeDtypeStruct((8, 8, 128), F32),
            jax.ShapeDtypeStruct((6, 8, 128), F32),
        ),
        in_specs=[sm] * 4 + [vm] * 6,
        out_specs=(vm, vm),
        scratch_shapes=[
            pltpu.VMEM((n_age, 8 * steps, 128), F32),
            pltpu.VMEM((n_plane, 8 * steps, 128), F32),
            pltpu.VMEM((6, 128 * n_plane, 128), F32),
            pltpu.VMEM((8, 8, 128), F32),
            pltpu.VMEM((steps, 8, 8, 128), F32),
            pltpu.VMEM((steps + 2, 8, 128), F32),
            pltpu.VMEM((steps, 8, 128), F32),
            pltpu.VMEM((steps + 1, 4, 8, 128), F32),
            pltpu.VMEM((steps, 2, 8, 8, 128), F32),
            pltpu.VMEM((6, 8, 128), F32),
            pltpu.VMEM((3, entries, 128), F32),
            dma((n_age,)),
            dma((n_age,)),
            dma((n_plane,)),
            dma((n_plane,)),
            dma((steps + 1, 7)),
            dma((steps + 1, 6)),
            dma((steps, 9)),
            dma((steps, 9)),
        ] + [pltpu.VMEM((empty + 1, 8, 128), F32)] * steps,
        compiler_params=pltpu.CompilerParams(
            collective_id=0, has_side_effects=True, vmem_limit_bytes=40 * 1024 * 1024
        ),
    )(
        az_index,
        free_stream,
        src,
        tgt,
        hot,
        surface_mu.reshape(az_dev, 128, 64),
        centroid_body.reshape(3, 128, 64),
        area_normal.reshape(3, 128, 64),
        te_body.reshape(3, 128),
        wake_state.reshape(8, 8, 128),
    )
    return (
        final.reshape(4, blades, tiles, 1, 128),
        vel.reshape(3, blades, tiles, 1, 128),
    )


def solution(mesh):
    in_specs = (
        P(("groups", "age"), "blade", None, "span"),
        P(None, "blade", None, "span"),
        P(None, "blade", None, "span"),
        P(None, "blade", "span"),
        P(None, "blade", ("groups", "age"), "span", None),
        P("blade", ("groups", "age"), "span", None),
        P("groups"),
        P("groups"),
    )
    out_specs = (
        P(None, "blade", ("groups", "age"), "span", None),
        P(None, "blade", ("groups", "age"), "span", None),
    )
    return jax.shard_map(
        on_device, mesh=mesh, in_specs=in_specs, out_specs=out_specs, check_vma=False
    )
```

time: 258 us -> 115 us (0.45)
  Pallas kernels: 0 us -> 107 us
  other arithmetic: 91.1 us -> 0.92 us
  starting transfers between devices: 77.3 us -> 0 us
  blocking collectives: 34.4 us -> 0 us
  waiting for transfers between devices: 20.1 us -> 0 us
  between operations: 11.3 us -> 0.72 us
  local copies, waits for them, and re-layouts: 16.5 us -> 6.04 us
  loops' own time: 5.87 us -> 0 us
    pallas_call x0 -> x1, Pallas kernels: none -> 107 us  [on_device(): pl.pallas_call(functools.partial(wake_kernel, (n_age, n_span, n_blade, st...]
    ppermute x27 -> x0, starting transfers between devices: 77.3 us -> none  [the longest x12 49.9 us: with_halo(): lax.ppermute(tail, axis, [(i, (i + 1) % count) for i in range(ends)])]
    reduce_sum x196 -> x2, other arithmetic: 44.1 us -> 0.22 us  [the longest x1 0.11 us: on_device(): tgt = jnp.sum(jnp.where(chosen, order[None, :] // slots, 0), axis=1)]
    sub x104 -> x0, other arithmetic: 24 us -> none  [the longest x48 14.4 us: near_velocity(): strengths[1][None, :] * separation[2]]
    all_gather x4 -> x0, blocking collectives: 21 us -> none  [the longest x3 15.9 us: on_device(): lax.all_gather(moment_got, ('span', 'blade'), axis=1, tiled=True)]
    ppermute x27 -> x0, waiting for transfers between devices: 20.1 us -> none  [the longest x12 10.2 us: with_halo(): lax.ppermute(head, axis, [((i + 1) % count, i) for i in range(ends)])]
    psum x1 -> x0, blocking collectives: 13.3 us -> none  [spread(): return lax.psum(jnp.where(mine, shard, jnp.zeros_like(shard)), axis)]
    div x49 -> x0, other arithmetic: 9.18 us -> none  [the longest x48 9.17 us: near_velocity(): weight = 1.0 / (dist_sq * jnp.sqrt(dist_sq))]
  transfers between devices with their start and end apart: 27 -> 0, of which waited for: 14 -> 0; matrix products, arithmetic and copies ran while one was open for 15% -> 0% of each run, Pallas kernels for 0% -> 0%
where the time goes in v1:
time: 115 us
  Pallas kernels  107 us (93%)
  local copies, waits for them, and re-layouts  6.04 us (5%)
    pallas_call x1, Pallas kernels, on_device(): pl.pallas_call(functools.partial(wake_kernel, (n_age, n_span, n_blade, st...  107 us
    unnamed x17, local copies, waits for them, and re-layouts  5.18 us

profile of v1, /device:TPU:0, one launch (start us, length us, event | category | flops | bytes accessed | tf_op | source)
XLA Modules:
  0.0 114.9 jit_solution(10145976423935984930)
XLA Ops:
  0.6 0.0 copy-start.6
  0.6 0.0 copy-start.3
  0.7 0.8 reshape.141.te_ref
  1.4 0.5 broadcast.144
  1.9 0.0 copy-done.6
  1.9 0.7 reduce.3
  2.6 0.1 reshape.137
  2.7 0.1 convert_reduce_fusion
  2.9 0.1 select_reduce_fusion
  3.0 0.0 copy-start.4
  3.0 0.0 copy-start.5
  3.0 0.0 copy-done.3
  3.0 0.6 copy-done.4
  3.6 0.0 copy-done.5
  3.7 0.0 copy-start
  3.7 0.9 copy-done
  4.6 0.0 copy-start.1
  4.6 0.9 copy-done.1
  5.5 0.0 copy-start.2
  5.5 0.9 copy-done.2
  6.5 107.2 %shard_map.95 = (f32[8,8,128]{2,1,0:T(8,128)S(1)}, f32[6,8,128]{2,1,0:T(8,128)S(1)}) custom-call(s32[3]{0:T(128)S(1)} %copy-done.4, f32[3]{0:T(128)S(1)} %copy-done.5, s32[64]{0:T(128)S(1)} %broadcast_add_fusion.src_ref, s32[64]{0:T(128)S(1)} %get-tuple-element.10.tgt_ref, f32[16,64]{1,0:T(8,128)S(1)} %fusion.2.hot_ref, f32[4,128,64]{2,1,0:T(8,128)S(1)} %bitcast.10, ...), custom_call_target="tpu_custom_call" | custom-call | tf_op jit(solution)/shard_map/pallas_call | solution.py:425
  113.7 0.6 copy.16
  114.3 0.6 copy.17
  (4 shorter events, 0.0 us)
Async XLA Ops:
  0.6 1.3 %copy-start.6 = (s32[2,8,1,8]{3,2,1,0:T(1,128)S(1)}, s32[2,8,1,8]{3,2,1,0:T(1,128)}, u32[]{:S(2)}) copy-start(s32[2,8,1,8]{3,2,1,0:T(1,128)} %param.13) | copy-start | bytes 1540
  0.6 2.4 %copy-start.3 = (f32[4,2,8,1,128]{4,3,2,1,0:T(1,128)S(1)}, f32[4,2,8,1,128]{4,3,2,1,0:T(1,128)}, u32[]{:S(2)}) copy-start(f32[4,2,8,1,128]{4,3,2,1,0:T(1,128)} %param.12) | copy-start | bytes 98308
  3.0 0.7 copy-start.4
  3.0 0.7 copy-start.5
  3.7 0.9 copy-start
  4.6 0.9 copy-start.1
  5.5 0.9 copy-start.2

commit v2 on v1

--- a/solution.py
+++ b/solution.py
@@ -27,7 +27,7 @@
     az_ref, fs_ref, src_ref, tgt_ref,
     hot_ref, mu_ref, cen_ref, nrm_ref, te_ref, state_ref,
     final_ref, vel_ref,
-    g1, g2, srcs, cur, moved, tile_out, shed, tail_in, side_in, far_out, near_out,
+    g1, g2, srcs, cur, moved, tile_out, shed, tail_in, side_in, far_out, near_out, goals,
     g1_send, g1_recv, g2_send, g2_recv, a_send, a_recv, b_send, b_recv, *tables,
 ):
     n_age, n_span, n_blade, steps, az_dev = sizes
@@ -291,28 +291,63 @@
 
         lax.fori_loop(0, 2, per_blade, 0)
 
+    def fill_goals(k):
+        def body(t, carry):
+            cols = jnp.transpose(tables[k][64 + t])
+            for c in range(3):
+                for g in range(16):
+                    goals[c, 16 * t + g] = jnp.broadcast_to(cols[8 * g:8 * g + 8, c:c + 1], (8, 128))
+            return carry
+
+        lax.fori_loop(0, 16, body, 0, unroll=4)
+
     def near(k):
         def body(e, carry):
             s = src_ref[e]
-            t = tgt_ref[e]
-            cols = jnp.transpose(tables[k][s])
-            goal_tile = tables[k][64 + t]
-            goal = [jnp.broadcast_to(goal_tile[c:c + 1], (8, 128)) for c in range(3)]
-            acc = [jnp.zeros((8, 128), F32) for _ in range(3)]
+            base = tgt_ref[e] * 16
+            tile = tables[k][s]
+            p = [tile[c:c + 1] for c in range(3)]
+            st = [tile[3 + c:4 + c] for c in range(3)]
+            wide = [jnp.broadcast_to(v, (8, 128)) for v in p]
+            parts = []
             for g in range(16):
-                part = cols[8 * g:8 * g + 8, :]
-                px, py, pz, sx, sy, sz = [jnp.broadcast_to(part[:, i:i + 1], (8, 128)) for i in range(6)]
-                dx, dy, dz = goal[0] - px, goal[1] - py, goal[2] - pz
+                dx, dy, dz = [goals[c, base + g] - wide[c] for c in range(3)]
                 r = lax.rsqrt(dx * dx + dy * dy + (dz * dz + NEAR_CORE))
-                w = r * r * r
-                acc[0] += w * (sy * dz - sz * dy)
-                acc[1] += w * (sz * dx - sx * dz)
-                acc[2] += w * (sx * dy - sy * dx)
-            for c in range(3):
-                near_out[c, pl.ds(e, 1), :] = jnp.sum(acc[c], axis=0, keepdims=True)
+                parts.append(r * r * r)
+            weight = jnp.concatenate(parts, axis=0)
+            qx, qy, qz = [p[c] - goals[c, base][0:1] for c in range(3)]
+            rows = st + [
+                st[1] * qz - st[2] * qy, st[2] * qx - st[0] * qz, st[0] * qy - st[1] * qx,
+                jnp.zeros((2, 128), F32)]
+            def split(v):
+                hi = v.astype(jnp.bfloat16)
+                rest = v - hi.astype(F32)
+                mid = rest.astype(jnp.bfloat16)
+                return hi, mid, (rest - mid.astype(F32)).astype(jnp.bfloat16)
+
+            stack = jnp.concatenate([v.astype(F32) for v in split(jnp.concatenate(rows, axis=0))], axis=0)
+            stack = stack.astype(jnp.bfloat16)
+            full = sum(
+                lax.dot_general(stack, v, (((1,), (1,)), ((), ())), preferred_element_type=F32)
+                for v in split(weight))
+            out = full[0:8] + full[8:16] + full[16:24]
+            for i in range(6):
+                near_out[i, pl.ds(e, 1), :] = out[i:i + 1]
             return carry
 
-        lax.fori_loop(0, entries, body, 0)
+        lax.fori_loop(0, entries, body, 0, unroll=8)
+
+    def close(k):
+        hot = hot_ref[...]
+        sums = [dot(hot, near_out[i]) for i in range(6)]
+        result = [[None, None] for _ in range(3)]
+        for b in range(2):
+            a = [sums[i][8 * b:8 * b + 8] for i in range(6)]
+            x = [cur[2 * c + b] - cur[2 * c + b, :, 0:1] for c in range(3)]
+            result[0][b] = a[1] * x[2] - a[2] * x[1] - a[3]
+            result[1][b] = a[2] * x[0] - a[0] * x[2] - a[4]
+            result[2][b] = a[0] * x[1] - a[1] * x[0] - a[5]
+        return result
 
     plan = edge_plan(0)
     start(plan)
@@ -372,13 +407,13 @@
             blocks = block_plan(k)
             start(blocks)
         far(0)
+        fill_goals(k)
         finish(blocks)
         near(k)
-        hot = hot_ref[...]
+        beside = close(k)
         for c in range(3):
-            close = dot(hot, near_out[c])
             for b in range(2):
-                v = fs_ref[c] + far_out[2 * c + b] + close[8 * b:8 * b + 8]
+                v = fs_ref[c] + far_out[2 * c + b] + beside[c][b]
                 if k == steps - 1:
                     vel_ref[2 * c + b] = v
                 moved[k, 2 * c + b] = cur[2 * c + b] + STEP * v
@@ -441,7 +476,8 @@
             pltpu.VMEM((steps + 1, 4, 8, 128), F32),
             pltpu.VMEM((steps, 2, 8, 8, 128), F32),
             pltpu.VMEM((6, 8, 128), F32),
-            pltpu.VMEM((3, entries, 128), F32),
+            pltpu.VMEM((6, entries, 128), F32),
+            pltpu.VMEM((3, 16 * 16, 8, 128), F32),
             dma((n_age,)),
             dma((n_age,)),
             dma((n_plane,)),

time: 115 us -> 67.2 us (0.58)
  Pallas kernels: 107 us -> 59.2 us
    pallas_call x1, Pallas kernels: 107 us -> 59.2 us  [on_device(): pl.pallas_call(functools.partial(wake_kernel, (n_age, n_span, n_blade, st...]
where the time goes in v2:
time: 67.2 us; the launch traced here: 66.9 us
  Pallas kernels  59.2 us (88%)
  local copies, waits for them, and re-layouts  6.04 us (9%)
  other arithmetic  0.92 us (1%)
  between operations  0.72 us (1%)
    pallas_call x1, Pallas kernels, on_device(): pl.pallas_call(functools.partial(wake_kernel, (n_age, n_span, n_blade, st...  59.2 us
    unnamed x17, local copies, waits for them, and re-layouts  5.18 us

profile of v2, /device:TPU:0, one launch (start us, length us, event | category | flops | bytes accessed | tf_op | source)
XLA Modules:
  0.0 66.9 jit_solution(6630759178578638630)
XLA Ops:
  0.6 0.0 copy-start.6
  0.6 0.0 copy-start.3
  0.7 0.8 %reshape.141.te_ref = f32[3,128]{1,0:T(4,128)S(1)} reshape(f32[3,2,64]{2,1,0:T(2,128)} %param.11) | data formatting | bytes 3072 | tf_op jit(solution)/shard_map/reshape | solution.py:502
  1.4 0.5 broadcast.144
  1.9 0.0 copy-done.6
  1.9 0.7 %reduce.3 = s32[2,8,8]{2,1,0:T(8,128)S(1)} reduce(s32[2,8,1,8]{3,2,1,0:T(1,128)S(1)} %copy-done.6, s32[]{:T(128)} %broadcast.144), dimensions={2}, to_apply=%param.13.reduce_sub_computation.3 | reduce | bytes 1028 | tf_op args[5]
  2.6 0.1 reshape.137
  2.7 0.1 convert_reduce_fusion
  2.9 0.1 select_reduce_fusion
  3.0 0.0 copy-start.4
  3.0 0.0 copy-start.5
  3.0 0.0 copy-done.3
  3.0 0.6 copy-done.4
  3.6 0.0 copy-done.5
  3.7 0.0 copy-start
  3.7 0.9 %copy-done = f32[4,2,64,64]{3,2,1,0:T(8,128)S(1)} copy-done((f32[4,2,64,64]{3,2,1,0:T(8,128)S(1)}, f32[4,2,64,64]{3,2,1,0:T(8,128)}, u32[]{:S(2)}) %copy-start) | copy-done | bytes 131096
  4.6 0.0 copy-start.1
  4.6 0.9 %copy-done.1 = f32[3,2,64,64]{3,2,1,0:T(8,128)S(1)} copy-done((f32[3,2,64,64]{3,2,1,0:T(8,128)S(1)}, f32[3,2,64,64]{3,2,1,0:T(8,128)}, u32[]{:S(2)}) %copy-start.1) | copy-done | bytes 98328
  5.5 0.0 copy-start.2
  5.5 0.9 %copy-done.2 = f32[3,2,64,64]{3,2,1,0:T(8,128)S(1)} copy-done((f32[3,2,64,64]{3,2,1,0:T(8,128)S(1)}, f32[3,2,64,64]{3,2,1,0:T(8,128)}, u32[]{:S(2)}) %copy-start.2) | copy-done | bytes 98328
  6.5 59.2 %shard_map.95 = (f32[8,8,128]{2,1,0:T(8,128)S(1)}, f32[6,8,128]{2,1,0:T(8,128)S(1)}) custom-call(s32[3]{0:T(128)S(1)} %copy-done.4, f32[3]{0:T(128)S(1)} %copy-done.5, s32[64]{0:T(128)S(1)} %broadcast_add_fusion.src_ref, s32[64]{0:T(128)S(1)} %get-tuple-element.10.tgt_ref, f32[16,64]{1,0:T(8,128)S(1)} %fusion.2.hot_ref, f32[4,128,64]{2,1,0:T(8,128)S(1)} %bitcast.10, ...), custom_call_target="tpu_custom_call" | custom-call | tf_op jit(solution)/shard_map/pallas_call | solution.py:460
  65.7 0.6 copy.16
  66.3 0.6 copy.17
  (4 shorter events, 0.0 us)
Async XLA Ops:
  0.6 1.3 %copy-start.6 = (s32[2,8,1,8]{3,2,1,0:T(1,128)S(1)}, s32[2,8,1,8]{3,2,1,0:T(1,128)}, u32[]{:S(2)}) copy-start(s32[2,8,1,8]{3,2,1,0:T(1,128)} %param.13) | copy-start | bytes 1540
  0.6 2.4 %copy-start.3 = (f32[4,2,8,1,128]{4,3,2,1,0:T(1,128)S(1)}, f32[4,2,8,1,128]{4,3,2,1,0:T(1,128)}, u32[]{:S(2)}) copy-start(f32[4,2,8,1,128]{4,3,2,1,0:T(1,128)} %param.12) | copy-start | bytes 98308
  3.0 0.7 copy-start.4
  3.0 0.7 copy-start.5
  3.7 0.9 %copy-start = (f32[4,2,64,64]{3,2,1,0:T(8,128)S(1)}, f32[4,2,64,64]{3,2,1,0:T(8,128)}, u32[]{:S(2)}) copy-start(f32[4,2,64,64]{3,2,1,0:T(8,128)} %param.8) | copy-start | bytes 393220
  4.6 0.9 %copy-start.1 = (f32[3,2,64,64]{3,2,1,0:T(8,128)S(1)}, f32[3,2,64,64]{3,2,1,0:T(8,128)}, u32[]{:S(2)}) copy-start(f32[3,2,64,64]{3,2,1,0:T(8,128)} %param.9) | copy-start | bytes 294916
  5.5 0.9 %copy-start.2 = (f32[3,2,64,64]{3,2,1,0:T(8,128)S(1)}, f32[3,2,64,64]{3,2,1,0:T(8,128)}, u32[]{:S(2)}) copy-start(f32[3,2,64,64]{3,2,1,0:T(8,128)} %param.10) | copy-start | bytes 294916
